TPU v7x, 32 devices: a whole 2x2x4 slice. The times are simulated.
32 devices in a mesh: grp: 2 (over x), head: 16 (over z, y, core).
Axes of the slice: x: 2, y: 2, z: 4, core: 2. Of those that a mesh axis runs over, the one named last changes fastest.
Arguments:
- tokens: bfloat16 [256, 16384], P('grp', 'head'), parts along dimension 0, may hold values from -14 to 14
- positions: int32 [256], P('grp'), parts along dimension 0, may hold values from 0 to 127, each once
- q_weight: bfloat16 [16384, 2048], P(None, 'head'), may hold values from -0.046875 to 0.046875
- kv_weight: bfloat16 [16384, 256], P('head'), may hold values from -0.046875 to 0.046875
- o_weight: bfloat16 [2048, 16384], P('head'), may hold values from -0.125 to 0.125
Outputs:
- attended: bfloat16 [256, 16384], P('grp', 'head'), parts along dimension 0
There are 2 independent parts, one for each index of `grp`. A program takes and returns all parts, laid end to end along the dimension named above; an argument that names none is the same for every part. Nothing has to cross between parts.
Inputs may be any that keep to these rules, and one draw needn't show every extreme that they name: `positions`: each of 0 to 127 appears exactly once.
All inputs are finite; a program needn't handle non-finite values.
Results may differ from a plain program's by a relative error of at most 0.012.
The roundings to bfloat16 on the way count: a program that leaves them out, or rounds other values in their place, can miss the bound.
Values may be sent and summed in bfloat16 or wider, within the bound.
A program may use at most 64 MiB of HBM per device.

v0:
```python
import jax
import jax.numpy as jnp
from jax import lax
from jax.sharding import PartitionSpec as P

HD = 128
GROUP = 16


def rotate(vals, positions):
    half = vals.shape[-1] // 2
    inverse = 500000.0 ** (-(jnp.arange(half, dtype=jnp.float32) * 2.0 / vals.shape[-1]))
    angles = positions.astype(jnp.float32)[:, None] * inverse[None, :]
    cosine = jnp.cos(angles)[:, None, :]
    sine = jnp.sin(angles)[:, None, :]
    first = vals[..., :half]
    second = vals[..., half:]
    return jnp.concatenate(
        [first * cosine - second * sine, second * cosine + first * sine], axis=-1
    )


def on_device(tokens, positions, q_weight, kv_weight, o_weight):
    count_tok = tokens.shape[0]
    width = q_weight.shape[1]
    head_size = HD
    local_heads = width // head_size
    kv_width = kv_weight.shape[1]
    kv_half = kv_width // 2
    first_head = lax.axis_index("head") * local_heads
    kv_index = first_head // GROUP
    q_raw = jnp.dot(
        lax.all_gather(tokens, "head", axis=1, tiled=True),
        q_weight,
        preferred_element_type=jnp.float32,
    )
    partial_value = jnp.dot(tokens, kv_weight, preferred_element_type=jnp.float32)
    kv_raw = lax.psum(partial_value, "head")
    k_raw = lax.dynamic_slice_in_dim(kv_raw, kv_index * head_size, head_size, 1)
    v_raw = lax.dynamic_slice_in_dim(kv_raw, kv_half + kv_index * head_size, head_size, 1)
    queries = rotate(q_raw.reshape(count_tok, local_heads, head_size), positions).astype(
        jnp.bfloat16
    )
    keys = rotate(k_raw.reshape(count_tok, 1, head_size), positions)[:, 0, :].astype(jnp.bfloat16)
    values = v_raw.astype(jnp.bfloat16)
    scores = jnp.einsum(
        "qhd,kd->hqk", queries, keys, preferred_element_type=jnp.float32
    ) / jnp.sqrt(jnp.float32(head_size))
    allowed = positions[None, :] <= positions[:, None]
    scores = jnp.where(allowed[None], scores, -1e30)
    peak = jnp.max(scores, axis=-1, keepdims=True)
    expo = jnp.where(allowed[None], jnp.exp(scores - peak), 0.0)
    weights = (expo / jnp.sum(expo, axis=-1, keepdims=True)).astype(jnp.bfloat16)
    context = jnp.einsum("hqk,kd->qhd", weights, values, preferred_element_type=jnp.float32)
    context = context.astype(jnp.bfloat16).reshape(count_tok, width)
    summed = lax.psum_scatter(
        lax.dot_general(
            o_weight, context, (((0,), (1,)), ((), ())), preferred_element_type=jnp.float32
        ),
        "head",
        scatter_dimension=0,
        tiled=True,
    ).T
    return summed.astype(jnp.bfloat16)


def solution(mesh):
    return jax.shard_map(
        on_device,
        mesh=mesh,
        in_specs=(P("grp", "head"), P("grp"), P(None, "head"), P("head", None), P("head", None)),
        out_specs=P("grp", "head"),
        check_vma=False,
    )
```

profile of v0, /device:TPU:0, one launch (start us, length us, event | category | flops | bytes accessed | tf_op | source)
XLA Modules:
  0.0 279.4 jit_solution(9040317520246895840)
XLA Ops:
  6.5 0.0 copy-start
  6.5 0.0 all-reduce.2.cloned.1.call-start
  6.5 1.0 copy-done
  7.6 1.8 fusion.44
  9.4 0.0 all-reduce.2.cloned.1.call-update
  9.4 0.0 all-gather.2.cloned.1.call-start
  9.5 0.7 all-gather.2.cloned.1.call-update
  10.2 0.0 reduce-scatter.2.cloned.1.call-start
  10.3 0.7 convert_element_type.34
  10.9 89.5 %all-reduce.2.cloned.1.call-done = f32[128,256]{1,0:T(8,128)} async-done(((f32[128,256]{1,0:T(8,128)}), f32[128,256]{1,0:T(8,128)}) %all-reduce.2.cloned.1.call-update) | async-done | bytes 131088 | tf_op jit(solution)/shard_map/psum | solution.py:38
  100.5 0.8 dynamic-slice_bitcast_fusion
  101.3 0.1 fusion.42
  101.4 0.1 copy.9
  101.4 0.1 copy.8
  101.5 0.0 copy-start.1
  101.6 53.3 %all-gather.2.cloned.1.call-done = bf16[128,16384]{1,0:T(8,128)(2,1)} async-done(((bf16[128,1024]{1,0:T(8,128)(2,1)}), bf16[128,16384]{1,0:T(8,128)(2,1)}) %all-gather.2.cloned.1.call-update) | async-done | bytes 4194320 | tf_op jit(solution)/shard_map/all_gather | solution.py:33
  154.9 5.2 %convolution_bitcast_fusion.1 = f32[128,1,128]{0,2,1:T(8,128)S(1)} fusion(bf16[128,16384]{1,0:T(8,128)(2,1)} %all-gather.2.cloned.1.call-done, bf16[16384,128]{1,0:T(8,128)(2,1)} %param.7), kind=kOutput, calls=%fused_computation.3 | convolution fusion | flops 536870912 | bytes 8454144 | tf_op jit(solution)/shard_map/dot_general | solution.py:32
  160.1 0.2 fusion.36
  160.3 0.0 copy-done.1
  160.3 0.2 fusion.43
  160.5 0.1 fusion.3
  160.6 6.9 %convolution_bitcast_fusion = f32[16384,128]{0,1:T(8,128)} fusion(bf16[128,16384]{1,0:T(8,128)(2,1)} %param.9, f32[128,256]{1,0:T(8,128)} %all-reduce.2.cloned.1.call-done, s32[]{:T(128)S(6)} %select_n.19, f32[1,128,128]{1,2,0:T(8,128)S(1)} %get-tuple-element.14, f32[128]{0:T(128)S(1)} %fusion.3, f32[128]{0:T(128)S(1)} %get-tuple-element.13, s32[128]{0:T(128)S(1)} %copy-done.1), kind=kOutput, calls=%fused_computation | convolution fusion | flops 541163520 | bytes 12683268 | tf_op jit(solution)/shard_map/dot_general | solution.py:57
  167.6 0.0 reduce-scatter.2.cloned.1.call-update
  167.6 103.5 %reduce-scatter.2.cloned.1.call-done = f32[1024,128]{0,1:T(8,128)} async-done(((f32[16384,128]{0,1:T(8,128)}), f32[1024,128]{0,1:T(8,128)}) %reduce-scatter.2.cloned.1.call-update) | async-done | bytes 524304 | tf_op jit(solution)/shard_map/reduce_scatter | solution.py:56
  271.1 1.8 convert_bitcast_fusion
  (1 shorter events, 0.0 us)
Async XLA Ops:
  6.5 1.0 copy-start
  6.5 93.9 %all-reduce.2.cloned.1.call-start = ((), (), s32[]{:S(2)}) async-start(), calls=%async_computation.1 | async-start | bytes 262144 | tf_op jit(solution)/shard_map/psum | solution.py:38
  9.4 145.5 %all-gather.2.cloned.1.call-start = ((), (), s32[]{:S(2)}) async-start(), calls=%async_computation.2 | async-start | bytes 4456448 | tf_op jit(solution)/shard_map/all_gather | solution.py:33
  10.2 260.9 %reduce-scatter.2.cloned.1.call-start = ((), (), s32[]{:S(2)}) async-start(), calls=%async_computation.3 | async-start | bytes 8912896 | tf_op jit(solution)/shard_map/reduce_scatter | solution.py:56
  101.5 58.8 %copy-start.1 = (s32[128]{0:T(128)S(1)}, s32[128]{0:T(128)}, u32[]{:S(2)}) copy-start(s32[128]{0:T(128)} %param.6) | copy-start | bytes 1540
Sparse Core Ops, SparseCore 0:
  10.8 89.6 all-reduce.1
  102.6 52.2 all-gather.1
  167.7 103.3 reduce-scatter.1
where the time goes:
time: 280 us; the launch traced here: 279 us
  waiting for transfers between devices  247 us (88%)
  matrix products  14.2 us (5%)
  between operations  13.2 us (5%)
    reduce_scatter x1, waiting for transfers between devices, on_device(): lax.psum_scatter(lax.dot_general(o_weight, context, (((0,), (1,)), ((), (...  103 us
    psum x1, waiting for transfers between devices, on_device(): kv_raw = lax.psum(partial_value, 'head')  89.5 us
    all_gather x1, waiting for transfers between devices, on_device(): lax.all_gather(tokens, 'head', axis=1, tiled=True)  53.3 us
    dot_general x1, matrix products, on_device(): lax.dot_general(o_weight, context, (((0,), (1,)), ((), ())), preferred_el...  6.95 us
  transfers between devices with their start and end apart: 3, of which 3 were waited for; matrix products, arithmetic and copies ran while one was open for 1% of the time, Pallas kernels for 0%

commit v1 on v0

--- a/solution.py
+++ b/solution.py
@@ -1,6 +1,10 @@
+import functools
+
 import jax
 import jax.numpy as jnp
 from jax import lax
+from jax.experimental import pallas as pl
+from jax.experimental.pallas import tpu as pltpu
 from jax.sharding import PartitionSpec as P
 
 HD = 128
@@ -64,9 +68,323 @@
     return summed.astype(jnp.bfloat16)
 
 
+RING = 8
+CORES = 2
+
+
+def head_at(place, core):
+    side = lax.div(place, RING // 2)
+    level = place * (1 - side) + (RING - 1 - place) * side
+    return (level * 2 + side) * CORES + core
+
+
+def fused(
+    cos_ref, sin_ref, pos_col, pos_row, tok_hbm, q_hbm, kv_hbm, o_hbm, out_ref,
+    tok, qw, kvw, ow, q_acc, q_send, q_recv, kv_part, kv_sib, kv_sum, kv_in, kv_all,
+    ctx, part, rs_send, rs_recv,
+    tok_sem, kvw_sem, q_sem, q_out, q_in, o_sem, o_out, o_in,
+    ag_out, ag_in, pair_out, pair_in, kr_out, kr_in, ka_out, ka_in, rs_out, rs_in,
+):
+    rows, width = out_ref.shape
+    half_w = width // 2
+    half_r = rows // 2
+    piece = rows // RING
+    me = lax.axis_index("head")
+    core = lax.rem(me, CORES)
+    chip = lax.div(me, CORES)
+    side = lax.rem(chip, 2)
+    level = lax.div(chip, 2)
+    place = level * (1 - side) + (RING - 1 - level) * side
+
+    def at(offset, which):
+        return head_at(lax.rem(place + offset + RING, RING), which)
+
+    sibling = chip * CORES + (1 - core)
+    right = at(1, core)
+    left = at(-1, core)
+
+    def push(src, dst, send, recv, target):
+        copy = pltpu.make_async_remote_copy(
+            src_ref=src, dst_ref=dst, send_sem=send, recv_sem=recv,
+            device_id={"head": target}, device_id_type=pl.DeviceIdType.MESH,
+        )
+        copy.start()
+        return copy
+
+    def pull(src, dst, sem):
+        copy = pltpu.make_async_copy(src, dst, sem)
+        copy.start()
+        return copy
+
+    sent = []
+    tok_local = [
+        pull(tok_hbm.at[:, pl.ds(b * half_w, half_w)], tok.at[0, b], tok_sem.at[b])
+        for b in range(2)
+    ]
+    kvw_local = pull(kv_hbm, kvw, kvw_sem)
+
+    barrier = pltpu.get_barrier_semaphore()
+    for offset in range(RING):
+        for other in range(CORES):
+            if offset or other:
+                pl.semaphore_signal(
+                    barrier, inc=1,
+                    device_id={"head": at(offset, lax.rem(core + other, CORES))},
+                    device_id_type=pl.DeviceIdType.MESH,
+                )
+    pl.semaphore_wait(barrier, RING * CORES - 1)
+
+    ways = (right, left)
+
+    def shard(way, hop):
+        return hop if way == 0 else (RING - hop) % RING
+
+    def ag_send(i):
+        for way in range(2):
+            b = (i + way) % 2
+            hop = i // 2
+            if hop == 0:
+                source = tok_hbm.at[:, pl.ds(b * half_w, half_w)]
+            else:
+                source = tok.at[shard(way, hop), b]
+            sent.append(push(
+                source, tok.at[shard(way, hop + 1), b],
+                ag_out.at[way, i], ag_in.at[way, i], ways[way],
+            ))
+
+    def ag_wait(i, way):
+        b = (i + way) % 2
+        slot = tok.at[shard(way, i // 2 + 1), b]
+        pltpu.make_async_remote_copy(
+            src_ref=slot, dst_ref=slot, send_sem=ag_out.at[way, i], recv_sem=ag_in.at[way, i],
+            device_id={"head": ways[1 - way]}, device_id_type=pl.DeviceIdType.MESH,
+        ).wait_recv()
+
+    def q_add(slot, b):
+        q_acc[...] += jnp.dot(
+            tok[slot, b], qw[slot, b * half_w:(b + 1) * half_w, :],
+            preferred_element_type=jnp.float32,
+        )
+
+    last = 2 * (RING // 2 - 1)
+    ag_send(0)
+    ag_send(1)
+
+    q_local, q_pair = [], []
+    for r in range(RING):
+        owner = lax.div(at(-r, core), CORES)
+        q_local.append(pull(q_hbm.at[owner, core], qw.at[r, :, 0:HD], q_sem.at[r]))
+        q_pair.append(push(
+            q_hbm.at[owner, 1 - core], qw.at[r, :, HD:2 * HD], q_out.at[r], q_in.at[r], sibling
+        ))
+    sent += q_pair
+
+    for copy in tok_local:
+        copy.wait()
+    kvw_local.wait()
+    both = jnp.dot(tok[0, 0], kvw[0:half_w, :], preferred_element_type=jnp.float32)
+    both += jnp.dot(tok[0, 1], kvw[half_w:width, :], preferred_element_type=jnp.float32)
+    kv_part[0] = both[:, 0:HD]
+    kv_part[1] = both[:, HD:2 * HD]
+    kv_pair = push(kv_part.at[1 - core], kv_sib, pair_out.at[0], pair_in.at[0], sibling)
+    sent.append(kv_pair)
+
+    def step(i):
+        for way in range(2):
+            ag_wait(i, way)
+        if i + 2 <= last:
+            ag_send(i + 2)
+
+    step(0)
+    kv_pair.wait_recv()
+    kv_sum[...] = (kv_part[core] + kv_sib[...]).reshape(RING, piece, HD)
+    kv_rows = []
+    for r in range(1, RING):
+        to = lax.rem(place + r, RING)
+        kv_rows.append(push(
+            kv_sum.at[to], kv_in.at[r], kr_out.at[r], kr_in.at[r], at(r, core)
+        ))
+    sent += kv_rows
+
+    step(1)
+    o_local, o_pair = [], []
+    for r in range(RING):
+        mine = pl.multiple_of(at(-r, core) * width, width)
+        theirs = pl.multiple_of(at(-r, 1 - core) * width, width)
+        o_local.append(pull(o_hbm.at[:, pl.ds(mine, width)], ow.at[r, 0:HD], o_sem.at[r]))
+        o_pair.append(push(
+            o_hbm.at[:, pl.ds(theirs, width)], ow.at[r, HD:2 * HD], o_out.at[r], o_in.at[r],
+            sibling,
+        ))
+    sent += o_pair
+    q_acc[...] = jnp.zeros_like(q_acc)
+    for r in range(RING):
+        q_local[r].wait()
+        q_pair[r].wait_recv()
+
+    for b in range(2):
+        q_add(0, b)
+    for i in range(2):
+        for way in range(2):
+            q_add(shard(way, i // 2 + 1), (i + way) % 2)
+
+    for i in range(2, last + 1):
+        step(i)
+        if i == 2:
+            total = kv_sum[place]
+            for r in range(1, RING):
+                kv_rows[r - 1].wait_recv()
+                total += kv_in[r]
+            turned = total * cos_ref[place] + pltpu.roll(total, HD // 2, 1) * sin_ref[place]
+            is_key = (core == 0).astype(jnp.float32)
+            kv_all[core, place] = (turned * is_key + total * (1.0 - is_key)).astype(jnp.bfloat16)
+            kv_out = []
+            for r in range(RING):
+                for other in range(CORES):
+                    if r or other:
+                        kv_out.append(push(
+                            kv_all.at[core, place], kv_all.at[core, place],
+                            ka_out.at[other, r], ka_in.at[other, r],
+                            at(r, lax.rem(core + other, CORES)),
+                        ))
+            sent += kv_out
+        for way in range(2):
+            q_add(shard(way, i // 2 + 1), (i + way) % 2)
+
+    q_send[...] = q_acc[:, HD:2 * HD]
+    q_pass = push(q_send, q_recv, pair_out.at[1], pair_in.at[1], sibling)
+    sent.append(q_pass)
+    for copy in kv_out:
+        copy.wait_recv()
+    q_pass.wait_recv()
+    q_raw = q_acc[:, 0:HD] + q_recv[...]
+    cosine = cos_ref[...].reshape(rows, HD)
+    sine = sin_ref[...].reshape(rows, HD)
+    queries = (q_raw * cosine + pltpu.roll(q_raw, HD // 2, 1) * sine).astype(jnp.bfloat16)
+    keys = kv_all[0].reshape(rows, HD)
+    values = kv_all[1].reshape(rows, HD)
+    scores = lax.dot_general(
+        queries, keys, (((1,), (1,)), ((), ())), preferred_element_type=jnp.float32
+    ) * (HD ** -0.5)
+    allowed = pos_row[...] <= pos_col[...]
+    scores = jnp.where(allowed, scores, -1e30)
+    peak = jnp.max(scores, axis=-1, keepdims=True)
+    expo = jnp.where(allowed, jnp.exp(scores - peak), 0.0)
+    weights = (expo / jnp.sum(expo, axis=-1, keepdims=True)).astype(jnp.bfloat16)
+    ctx[0] = jnp.dot(weights, values, preferred_element_type=jnp.float32).astype(jnp.bfloat16)
+    ctx_pass = push(ctx.at[0], ctx.at[1], pair_out.at[2], pair_in.at[2], sibling)
+    sent.append(ctx_pass)
+    for r in range(RING):
+        o_local[r].wait()
+        o_pair[r].wait_recv()
+    ctx_pass.wait_recv()
+
+    context = jnp.concatenate([ctx[0], ctx[1]], axis=1)
+    tile = 2 * HD
+
+    def project(slot):
+        for n in range(width // tile):
+            part[slot, :, n * tile:(n + 1) * tile] = jnp.dot(
+                context, ow[slot, :, n * tile:(n + 1) * tile], preferred_element_type=jnp.float32
+            )
+
+    def rs_wait(i, way):
+        slot = rs_recv.at[way, i]
+        pltpu.make_async_remote_copy(
+            src_ref=slot, dst_ref=slot, send_sem=rs_out.at[way, i], recv_sem=rs_in.at[way, i],
+            device_id={"head": ways[1 - way]}, device_id_type=pl.DeviceIdType.MESH,
+        ).wait_recv()
+
+    def rs_go(i):
+        hop = (i + 1) // 2
+        for way in range(2):
+            slot = RING // 2 + hop if way == 0 else RING // 2 - hop
+            b = (i + way) % 2
+            value = part[slot, b * half_r:(b + 1) * half_r, :]
+            if i >= 2:
+                rs_wait(i - 2, way)
+                value += rs_recv[way, i - 2].astype(jnp.float32)
+            rs_send[way, i] = value.astype(jnp.bfloat16)
+            sent.append(push(
+                rs_send.at[way, i], rs_recv.at[way, i], rs_out.at[way, i], rs_in.at[way, i],
+                ways[way],
+            ))
+
+    project(RING // 2)
+    rs_go(0)
+    for hop in range(1, RING // 2):
+        project(RING // 2 + hop)
+        project(RING // 2 - hop)
+        rs_go(2 * hop - 1)
+        if hop == RING // 2 - 1:
+            project(0)
+        rs_go(2 * hop)
+    for i in (last - 1, last):
+        for way in range(2):
+            b = (i + way) % 2
+            rs_wait(i, way)
+            part[0, b * half_r:(b + 1) * half_r, :] += rs_recv[way, i].astype(jnp.float32)
+    out_ref[...] = part[0].astype(out_ref.dtype)
+    for copy in sent:
+        copy.wait_send()
+
+
+def on_ring(tokens, positions, q_weight, kv_weight, o_weight):
+    rows, width = tokens.shape
+    half = HD // 2
+    inverse = 500000.0 ** (-(jnp.arange(half, dtype=jnp.float32) * 2.0 / HD))
+    angles = positions.astype(jnp.float32)[:, None] * inverse[None, :]
+    cosine, sine = jnp.cos(angles), jnp.sin(angles)
+    piece = rows // RING
+    cosine = jnp.concatenate([cosine, cosine], axis=1).reshape(RING, piece, HD)
+    sine = jnp.concatenate([-sine, sine], axis=1).reshape(RING, piece, HD)
+    hops = RING - 1
+    any_space = pl.BlockSpec(memory_space=pl.ANY)
+    vmem = pl.BlockSpec(memory_space=pltpu.VMEM)
+    bf16, f32 = jnp.bfloat16, jnp.float32
+    dma = pltpu.SemaphoreType.DMA
+    return pl.pallas_call(
+        fused,
+        out_shape=jax.ShapeDtypeStruct((rows, width), bf16),
+        in_specs=[vmem] * 4 + [any_space] * 4,
+        out_specs=vmem,
+        scratch_shapes=[
+            pltpu.VMEM((RING, 2, rows, width // 2), bf16),
+            pltpu.VMEM((RING, width, 2 * HD), bf16),
+            pltpu.VMEM((width, 2 * HD), bf16),
+            pltpu.VMEM((RING, 2 * HD, width), bf16),
+            pltpu.VMEM((rows, 2 * HD), f32),
+            pltpu.VMEM((rows, HD), f32),
+            pltpu.VMEM((rows, HD), f32),
+            pltpu.VMEM((2, rows, HD), f32),
+            pltpu.VMEM((rows, HD), f32),
+            pltpu.VMEM((RING, piece, HD), f32),
+            pltpu.VMEM((RING, piece, HD), f32),
+            pltpu.VMEM((2, RING, piece, HD), bf16),
+            pltpu.VMEM((2, rows, HD), bf16),
+            pltpu.VMEM((RING, rows, width), f32),
+            pltpu.VMEM((2, hops, rows // 2, width), bf16),
+            pltpu.VMEM((2, hops, rows // 2, width), bf16),
+            dma((2,)), dma, dma((RING,)), dma((RING,)), dma((RING,)),
+            dma((RING,)), dma((RING,)), dma((RING,)),
+            dma((2, hops)), dma((2, hops)), dma((3,)), dma((3,)),
+            dma((RING,)), dma((RING,)), dma((2, RING)), dma((2, RING)),
+            dma((2, hops)), dma((2, hops)),
+        ],
+        compiler_params=pltpu.CompilerParams(
+            collective_id=0, has_side_effects=True, vmem_limit_bytes=48 * 2**20
+        ),
+        name="prefill_ring",
+    )(
+        cosine, sine, positions[:, None], positions[None, :],
+        tokens, q_weight.reshape(RING, CORES, width, HD), kv_weight, o_weight,
+    )
+
+
 def solution(mesh):
+    ring = mesh.shape["head"] == RING * CORES
     return jax.shard_map(
-        on_device,
+        on_ring if ring else on_device,
         mesh=mesh,
         in_specs=(P("grp", "head"), P("grp"), P(None, "head"), P("head", None), P("head", None)),
         out_specs=P("grp", "head"),

time: 280 us -> 63.4 us (0.23)
  waiting for transfers between devices: 247 us -> 0 us
  Pallas kernels: 0 us -> 55.7 us
  matrix products: 14.2 us -> 0 us
  between operations: 13.2 us -> 0.04 us
  local copies, waits for them, and re-layouts: 2.13 us -> 6.38 us
    reduce_scatter x1 -> x0, waiting for transfers between devices: 103 us -> none  [on_device(): lax.psum_scatter(lax.dot_general(o_weight, context, (((0,), (1,)), ((), (...]
    psum x1 -> x0, waiting for transfers between devices: 89.5 us -> none  [on_device(): kv_raw = lax.psum(partial_value, 'head')]
    pallas_call x0 -> x1, Pallas kernels: none -> 55.7 us  [on_ring(): pl.pallas_call(fused, out_shape=jax.ShapeDtypeStruct((rows, width), bf16)...]
    all_gather x1 -> x0, waiting for transfers between devices: 53.3 us -> none  [on_device(): lax.all_gather(tokens, 'head', axis=1, tiled=True)]
    dot_general x4 -> x0, matrix products: 14.2 us -> none  [the longest x1 6.95 us: on_device(): lax.dot_general(o_weight, context, (((0,), (1,)), ((), ())), preferred_el...]
    unnamed x6 -> x9, local copies, waits for them, and re-layouts: 1.21 us -> 5.53 us
  transfers between devices with their start and end apart: 3 -> 0, of which waited for: 3 -> 0; matrix products, arithmetic and copies ran while one was open for 1% -> 0% of each run, Pallas kernels for 0% -> 0%
where the time goes in v1:
time: 63.4 us; the launch traced here: 63.2 us
  Pallas kernels  55.7 us (88%)
  local copies, waits for them, and re-layouts  6.38 us (10%)
  other arithmetic  1.07 us (2%)
    pallas_call x1, Pallas kernels, on_ring(): pl.pallas_call(fused, out_shape=jax.ShapeDtypeStruct((rows, width), bf16)...  55.7 us
    unnamed x9, local copies, waits for them, and re-layouts  5.53 us

profile of v1, /device:TPU:0, one launch (start us, length us, event | category | flops | bytes accessed | tf_op | source)
XLA Modules:
  0.0 63.2 jit_solution(6528290871987636087)
XLA Ops:
  0.0 0.7 %convert_element_type.3 = f32[128]{0:T(128)S(1)} convert(s32[128]{0:T(128)} %param.6) | non-fusion elementwise | flops 128 | bytes 1024 | tf_op jit(solution)/shard_map/convert_element_type | solution.py:336
  0.7 0.1 mul.22
  0.7 0.8 %copy.6.pos_col = s32[128,1]{1,0:T(8,128)S(1)} copy(s32[128,1]{0,1:T(1,128)} %bitcast.4) | data formatting | bytes 1024 | tf_op jit(solution)/shard_map/broadcast_in_dim | solution.py:379
  1.5 0.3 fusion
  1.8 0.1 pad_maximum_fusion
  1.9 0.0 copy-start
  1.9 2.2 %copy-done = bf16[16384,128]{1,0:T(8,128)(2,1)S(1)} copy-done((bf16[16384,128]{1,0:T(8,128)(2,1)S(1)}, bf16[16384,128]{1,0:T(8,128)(2,1)}, u32[]{:S(2)}) %copy-start) | copy-done | bytes 4194328
  4.1 0.0 copy-start.1
  4.1 1.0 %copy-done.1 = bf16[1024,256]{1,0:T(8,128)(2,1)S(1)} copy-done((bf16[1024,256]{1,0:T(8,128)(2,1)S(1)}, bf16[1024,256]{1,0:T(8,128)(2,1)}, u32[]{:S(2)}) %copy-start.1) | copy-done | bytes 524312
  5.2 0.0 copy-start.2
  5.2 0.9 %copy-done.2 = bf16[128,1024]{1,0:T(8,128)(2,1)S(1)} copy-done((bf16[128,1024]{1,0:T(8,128)(2,1)S(1)}, bf16[128,1024]{1,0:T(8,128)(2,1)}, u32[]{:S(2)}) %copy-start.2) | copy-done | bytes 262168
  6.1 0.0 copy-start.3
  6.1 0.7 %copy-done.3 = s32[128]{0:T(128)S(1)} copy-done((s32[128]{0:T(128)S(1)}, s32[128]{0:T(128)}, u32[]{:S(2)}) %copy-start.3) | copy-done | bytes 536
  6.8 55.7 %prefill_ring.1 = bf16[128,1024]{1,0:T(8,128)(2,1)S(1)} custom-call(f32[8,16,128]{2,1,0:T(8,128)S(1)} %get-tuple-element.8.cos_ref, f32[8,16,128]{2,1,0:T(8,128)S(1)} %get-tuple-element.9.sin_ref, s32[128,1]{1,0:T(8,128)S(1)} %copy.6.pos_col, s32[1,128]{1,0:T(1,128)S(1)} %bitcast.5, bf16[128,1024]{1,0:T(8,128)(2,1)S(1)} %copy-done.2, ...), custom_call_target="tpu_custom_call" | custom-call | tf_op jit(solution)/shard_map/prefill_ring/pallas_call | solution.py:346
  62.5 0.7 %copy.8 = bf16[128,1024]{1,0:T(8,128)(2,1)} copy(bf16[128,1024]{1,0:T(8,128)(2,1)S(1)} %prefill_ring.1) | data formatting | bytes 524288
  (1 shorter events, 0.0 us)
Async XLA Ops:
  1.9 2.2 %copy-start = (bf16[16384,128]{1,0:T(8,128)(2,1)S(1)}, bf16[16384,128]{1,0:T(8,128)(2,1)}, u32[]{:S(2)}) copy-start(bf16[16384,128]{1,0:T(8,128)(2,1)} %param.7) | copy-start | bytes 12582916
  4.1 1.0 %copy-start.1 = (bf16[1024,256]{1,0:T(8,128)(2,1)S(1)}, bf16[1024,256]{1,0:T(8,128)(2,1)}, u32[]{:S(2)}) copy-start(bf16[1024,256]{1,0:T(8,128)(2,1)} %kv_hbm.1) | copy-start | bytes 1572868
  5.2 0.9 %copy-start.2 = (bf16[128,1024]{1,0:T(8,128)(2,1)S(1)}, bf16[128,1024]{1,0:T(8,128)(2,1)}, u32[]{:S(2)}) copy-start(bf16[128,1024]{1,0:T(8,128)(2,1)} %tok_hbm.1) | copy-start | bytes 786436
  6.1 0.7 %copy-start.3 = (s32[128]{0:T(128)S(1)}, s32[128]{0:T(128)}, u32[]{:S(2)}) copy-start(s32[128]{0:T(128)} %param.6) | copy-start | bytes 1540

commit v2 on v1

--- a/solution.py
+++ b/solution.py
@@ -1,4 +1,4 @@
-import functools
+import math
 
 import jax
 import jax.numpy as jnp
@@ -79,10 +79,10 @@
 
 
 def fused(
-    cos_ref, sin_ref, pos_col, pos_row, tok_hbm, q_hbm, kv_hbm, o_hbm, out_ref,
+    pos_hbm, tok_hbm, q_hbm, kv_hbm, o_hbm, out_ref, pos, cos_ref, sin_ref,
     tok, qw, kvw, ow, q_acc, q_send, q_recv, kv_part, kv_sib, kv_sum, kv_in, kv_all,
     ctx, part, rs_send, rs_recv,
-    tok_sem, kvw_sem, q_sem, q_out, q_in, o_sem, o_out, o_in,
+    pos_sem, tok_sem, kvw_sem, q_sem, q_out, q_in, o_sem, o_out, o_in,
     ag_out, ag_in, pair_out, pair_in, kr_out, kr_in, ka_out, ka_in, rs_out, rs_in,
 ):
     rows, width = out_ref.shape
@@ -117,6 +117,7 @@
         return copy
 
     sent = []
+    pos_local = pull(pos_hbm, pos, pos_sem)
     tok_local = [
         pull(tok_hbm.at[:, pl.ds(b * half_w, half_w)], tok.at[0, b], tok_sem.at[b])
         for b in range(2)
@@ -178,6 +179,17 @@
             q_hbm.at[owner, 1 - core], qw.at[r, :, HD:2 * HD], q_out.at[r], q_in.at[r], sibling
         ))
     sent += q_pair
+
+    pos_local.wait()
+    pos_row = jnp.broadcast_to(pos[...].astype(jnp.float32), (rows, rows))
+    pos_col = pos_row.T
+    allowed = pos_row <= pos_col
+    lane = lax.broadcasted_iota(jnp.int32, (rows, HD), 1)
+    angle_step = lax.rem(lane, HD // 2).astype(jnp.float32) * (2.0 / HD)
+    angles = pos_col * jnp.exp(angle_step * -math.log(500000.0))
+    sine = jnp.sin(angles)
+    cos_ref[...] = jnp.cos(angles).reshape(RING, piece, HD)
+    sin_ref[...] = jnp.where(lane < HD // 2, -sine, sine).reshape(RING, piece, HD)
 
     for copy in tok_local:
         copy.wait()
@@ -266,7 +278,6 @@
     scores = lax.dot_general(
         queries, keys, (((1,), (1,)), ((), ())), preferred_element_type=jnp.float32
     ) * (HD ** -0.5)
-    allowed = pos_row[...] <= pos_col[...]
     scores = jnp.where(allowed, scores, -1e30)
     peak = jnp.max(scores, axis=-1, keepdims=True)
     expo = jnp.where(allowed, jnp.exp(scores - peak), 0.0)
@@ -331,24 +342,21 @@
 
 def on_ring(tokens, positions, q_weight, kv_weight, o_weight):
     rows, width = tokens.shape
-    half = HD // 2
-    inverse = 500000.0 ** (-(jnp.arange(half, dtype=jnp.float32) * 2.0 / HD))
-    angles = positions.astype(jnp.float32)[:, None] * inverse[None, :]
-    cosine, sine = jnp.cos(angles), jnp.sin(angles)
     piece = rows // RING
-    cosine = jnp.concatenate([cosine, cosine], axis=1).reshape(RING, piece, HD)
-    sine = jnp.concatenate([-sine, sine], axis=1).reshape(RING, piece, HD)
     hops = RING - 1
-    any_space = pl.BlockSpec(memory_space=pl.ANY)
+    any_space = pl.BlockSpec(memory_space=pltpu.HBM)
     vmem = pl.BlockSpec(memory_space=pltpu.VMEM)
     bf16, f32 = jnp.bfloat16, jnp.float32
     dma = pltpu.SemaphoreType.DMA
     return pl.pallas_call(
         fused,
         out_shape=jax.ShapeDtypeStruct((rows, width), bf16),
-        in_specs=[vmem] * 4 + [any_space] * 4,
+        in_specs=[any_space] * 5,
         out_specs=vmem,
         scratch_shapes=[
+            pltpu.VMEM((1, rows), jnp.int32),
+            pltpu.VMEM((RING, piece, HD), f32),
+            pltpu.VMEM((RING, piece, HD), f32),
             pltpu.VMEM((RING, 2, rows, width // 2), bf16),
             pltpu.VMEM((RING, width, 2 * HD), bf16),
             pltpu.VMEM((width, 2 * HD), bf16),
@@ -365,19 +373,18 @@
             pltpu.VMEM((RING, rows, width), f32),
             pltpu.VMEM((2, hops, rows // 2, width), bf16),
             pltpu.VMEM((2, hops, rows // 2, width), bf16),
-            dma((2,)), dma, dma((RING,)), dma((RING,)), dma((RING,)),
+            dma, dma((2,)), dma, dma((RING,)), dma((RING,)), dma((RING,)),
             dma((RING,)), dma((RING,)), dma((RING,)),
             dma((2, hops)), dma((2, hops)), dma((3,)), dma((3,)),
             dma((RING,)), dma((RING,)), dma((2, RING)), dma((2, RING)),
             dma((2, hops)), dma((2, hops)),
         ],
         compiler_params=pltpu.CompilerParams(
-            collective_id=0, has_side_effects=True, vmem_limit_bytes=48 * 2**20
+            collective_id=0, has_side_effects=True, vmem_limit_bytes=60 * 2**20
         ),
         name="prefill_ring",
     )(
-        cosine, sine, positions[:, None], positions[None, :],
-        tokens, q_weight.reshape(RING, CORES, width, HD), kv_weight, o_weight,
+        positions[None, :], tokens, q_weight.reshape(RING, CORES, width, HD), kv_weight, o_weight,
     )
 
 

time: 63.4 us -> 58.3 us (0.920)
  local copies, waits for them, and re-layouts: 6.38 us -> 1.67 us
  other arithmetic: 1.07 us -> 0 us
  Pallas kernels: 55.7 us -> 56.5 us
    unnamed x9 -> x1, local copies, waits for them, and re-layouts: 5.53 us -> 1.67 us
    pallas_call x1, Pallas kernels: 55.7 us -> 56.5 us  [on_ring(): pl.pallas_call(fused, out_shape=jax.ShapeDtypeStruct((rows, width), bf16)...]
    broadcast_in_dim x1 -> x0, local copies, waits for them, and re-layouts: 0.77 us -> none  [on_ring(): positions[:, None]]
    convert_element_type x1 -> x0, other arithmetic: 0.66 us -> none  [on_ring(): angles = positions.astype(jnp.float32)[:, None] * inverse[None, :]]
where the time goes in v2:
time: 58.3 us; the launch traced here: 58.2 us
  Pallas kernels  56.5 us (97%)
  local copies, waits for them, and re-layouts  1.67 us (3%)
    pallas_call x1, Pallas kernels, on_ring(): pl.pallas_call(fused, out_shape=jax.ShapeDtypeStruct((rows, width), bf16)...  56.5 us
    unnamed x1, local copies, waits for them, and re-layouts  1.67 us

profile of v2, /device:TPU:0, one launch (start us, length us, event | category | flops | bytes accessed | tf_op | source)
XLA Modules:
  0.0 58.2 jit_solution(12103891079046674717)
XLA Ops:
  0.0 56.5 %prefill_ring.1 = bf16[128,1024]{1,0:T(8,128)(2,1)} custom-call(s32[1,128]{1,0:T(1,128)} %bitcast.3, bf16[128,1024]{1,0:T(8,128)(2,1)} %tok_hbm.1, bf16[8,2,1024,128]{3,2,1,0:T(8,128)(2,1)} %bitcast.2, bf16[1024,256]{1,0:T(8,128)(2,1)} %kv_hbm.1, bf16[128,16384]{1,0:T(8,128)(2,1)} %o_hbm.1), custom_call_target="tpu_custom_call" | custom-call | tf_op jit(solution)/shard_map/prefill_ring/pallas_call | solution.py:351
  56.5 1.7 %copy.7 = bf16[128,1024]{1,0:T(8,128)(2,1)} copy(bf16[128,1024]{1,0:T(8,128)(2,1)} %prefill_ring.1) | data formatting | bytes 524288

commit v3 on v0

--- a/solution.py
+++ b/solution.py
@@ -1,6 +1,10 @@
+import math
+
 import jax
 import jax.numpy as jnp
 from jax import lax
+from jax.experimental import pallas as pl
+from jax.experimental.pallas import tpu as pltpu
 from jax.sharding import PartitionSpec as P
 
 HD = 128
@@ -64,9 +68,378 @@
     return summed.astype(jnp.bfloat16)
 
 
+RING = 8
+CORES = 2
+
+
+def head_at(place, core):
+    side = lax.div(place, RING // 2)
+    level = place * (1 - side) + (RING - 1 - place) * side
+    return (level * 2 + side) * CORES + core
+
+
+def fused(
+    pos_hbm, tok_hbm, q_hbm, kv_hbm, o_hbm, out_ref, pos, cos_ref, sin_ref,
+    tok, tok_own, qw, kvw, ow, q_acc, q_send, q_recv, kv_part, kv_sib, kv_sum, kv_in, kv_all,
+    ctx, part, rs_send, rs_recv,
+    pos_sem, tok_sem, kvw_sem, q_sem, q_out, q_in, o_sem, o_out, o_in,
+    ag_out, ag_in, pair_out, pair_in, qp_out, qp_in, cp_out, cp_in,
+    kr_out, kr_in, ka_out, ka_in, rs_out, rs_in,
+):
+    rows, width = out_ref.shape
+    half_w = width // 2
+    half_r = rows // 2
+    piece = rows // RING
+    me = lax.axis_index("head")
+    core = lax.rem(me, CORES)
+    chip = lax.div(me, CORES)
+    side = lax.rem(chip, 2)
+    level = lax.div(chip, 2)
+    place = level * (1 - side) + (RING - 1 - level) * side
+
+    def at(offset, which):
+        return head_at(lax.rem(place + offset + RING, RING), which)
+
+    sibling = chip * CORES + (1 - core)
+    right = at(1, core)
+    left = at(-1, core)
+
+    def push(src, dst, send, recv, target):
+        copy = pltpu.make_async_remote_copy(
+            src_ref=src, dst_ref=dst, send_sem=send, recv_sem=recv,
+            device_id={"head": target}, device_id_type=pl.DeviceIdType.MESH,
+        )
+        copy.start()
+        return copy
+
+    def pull(src, dst, sem):
+        copy = pltpu.make_async_copy(src, dst, sem)
+        copy.start()
+        return copy
+
+    sent = []
+    pos_local = pull(pos_hbm, pos, pos_sem)
+    tok_local = pull(tok_hbm, tok_own, tok_sem)
+    kvw_local = pull(kv_hbm, kvw, kvw_sem)
+
+    barrier = pltpu.get_barrier_semaphore()
+    for target in [sibling] + [at(offset, core) for offset in range(1, RING)]:
+        pl.semaphore_signal(
+            barrier, inc=1, device_id={"head": target}, device_id_type=pl.DeviceIdType.MESH
+        )
+    pl.semaphore_wait(barrier, RING)
+
+    ways = (right, left)
+
+    def shard(way, hop):
+        return hop if way == 0 else (RING - hop) % RING
+
+    def ag_send(h, i):
+        for way in range(2):
+            b = (i + way) % 2
+            hop = i // 2
+            if hop == 0:
+                source = tok_hbm.at[pl.ds(h * half_r, half_r), pl.ds(b * half_w, half_w)]
+            else:
+                source = tok.at[h, shard(way, hop), b]
+            sent.append(push(
+                source, tok.at[h, shard(way, hop + 1), b],
+                ag_out.at[h, way, i], ag_in.at[h, way, i], ways[way],
+            ))
+
+    def arrived(slot, send, recv, way):
+        pltpu.make_async_remote_copy(
+            src_ref=slot, dst_ref=slot, send_sem=send, recv_sem=recv,
+            device_id={"head": ways[1 - way]}, device_id_type=pl.DeviceIdType.MESH,
+        ).wait_recv()
+
+    last = 2 * (RING // 2 - 1)
+
+    def ag_step(h, i):
+        for way in range(2):
+            slot = tok.at[h, shard(way, i // 2 + 1), (i + way) % 2]
+            arrived(slot, ag_out.at[h, way, i], ag_in.at[h, way, i], way)
+        if i + 2 <= last:
+            ag_send(h, i + 2)
+        elif h == 0:
+            ag_send(1, i + 1 - last)
+
+    def q_add(h, i):
+        for way in range(2):
+            b = (i + way) % 2
+            slot = shard(way, i // 2 + 1)
+            q_acc[h] += jnp.dot(
+                tok[h, slot, b], qw[slot, b * half_w:(b + 1) * half_w, :],
+                preferred_element_type=jnp.float32,
+            )
+
+    ag_send(0, 0)
+    ag_send(0, 1)
+
+    q_local, q_pair = [], []
+    for r in range(RING):
+        owner = lax.div(at(-r, core), CORES)
+        q_local.append(pull(q_hbm.at[owner, core], qw.at[r, :, 0:HD], q_sem.at[r]))
+        q_pair.append(push(
+            q_hbm.at[owner, 1 - core], qw.at[r, :, HD:2 * HD], q_out.at[r], q_in.at[r], sibling
+        ))
+    sent += q_pair
+
+    tok_local.wait()
+    kvw_local.wait()
+    both = jnp.dot(tok_own[...], kvw[...], preferred_element_type=jnp.float32)
+    kv_part[0] = both[:, 0:HD]
+    kv_part[1] = both[:, HD:2 * HD]
+    kv_pair = push(kv_part.at[1 - core], kv_sib, pair_out.at[0], pair_in.at[0], sibling)
+    sent.append(kv_pair)
+
+    ag_step(0, 0)
+
+    pos_local.wait()
+    pos_row = jnp.broadcast_to(pos[...].astype(jnp.float32), (rows, rows))
+    pos_col = pos_row.T
+    lane = lax.broadcasted_iota(jnp.int32, (rows, HD), 1)
+    angle_step = lax.rem(lane, HD // 2).astype(jnp.float32) * (2.0 / HD)
+    angles = pos_col * jnp.exp(angle_step * -math.log(500000.0))
+    sine = jnp.sin(angles)
+    cos_ref[...] = jnp.cos(angles).reshape(RING, piece, HD)
+    sin_ref[...] = jnp.where(lane < HD // 2, -sine, sine).reshape(RING, piece, HD)
+
+    ag_step(0, 1)
+    kv_pair.wait_recv()
+    kv_sum[...] = (kv_part[core] + kv_sib[...]).reshape(RING, piece, HD)
+    kv_rows = []
+    for r in range(1, RING):
+        to = lax.rem(place + r, RING)
+        kv_rows.append(push(
+            kv_sum.at[to], kv_in.at[r], kr_out.at[r], kr_in.at[r], at(r, core)
+        ))
+    sent += kv_rows
+
+    o_local, o_pair = [], []
+    for r in range(RING):
+        mine = pl.multiple_of(at(-r, core) * width, width)
+        theirs = pl.multiple_of(at(-r, 1 - core) * width, width)
+        o_local.append(pull(o_hbm.at[:, pl.ds(mine, width)], ow.at[r, 0:HD], o_sem.at[r]))
+        o_pair.append(push(
+            o_hbm.at[:, pl.ds(theirs, width)], ow.at[r, HD:2 * HD], o_out.at[r], o_in.at[r],
+            sibling,
+        ))
+    sent += o_pair
+
+    ag_step(0, 2)
+    for r in range(RING):
+        q_local[r].wait()
+        q_pair[r].wait_recv()
+    own = jnp.dot(tok_own[...], qw[0], preferred_element_type=jnp.float32)
+    q_acc[0] = own[:half_r]
+    q_acc[1] = own[half_r:]
+    ag_step(0, 3)
+    for i in range(3):
+        q_add(0, i)
+    total = kv_sum[place]
+    for r in range(1, RING):
+        kv_rows[r - 1].wait_recv()
+        total += kv_in[r]
+    turned = total * cos_ref[place] + pltpu.roll(total, HD // 2, 1) * sin_ref[place]
+    is_key = (core == 0).astype(jnp.float32)
+    kv_all[core, place] = (turned * is_key + total * (1.0 - is_key)).astype(jnp.bfloat16)
+    kv_out = []
+    for r in range(1, RING):
+        kv_out.append(push(
+            kv_all.at[core, place], kv_all.at[core, place], ka_out.at[r], ka_in.at[r], at(r, core)
+        ))
+    sent += kv_out
+    ag_step(0, 4)
+    q_add(0, 3)
+    q_add(0, 4)
+    ag_step(0, 5)
+    q_add(0, 5)
+    for copy in kv_out:
+        copy.wait_recv()
+    kv_pass = push(kv_all.at[core], kv_all.at[core], pair_out.at[1], pair_in.at[1], sibling)
+    sent.append(kv_pass)
+    ag_step(0, 6)
+    q_add(0, 6)
+
+    def q_exchange(h):
+        q_send[h] = q_acc[h, :, HD:2 * HD]
+        copy = push(q_send.at[h], q_recv.at[h], qp_out.at[h], qp_in.at[h], sibling)
+        sent.append(copy)
+        return copy
+
+    def attend(h, q_pass):
+        q_pass.wait_recv()
+        lines = slice(h * half_r, (h + 1) * half_r)
+        q_raw = q_acc[h, :, 0:HD] + q_recv[h]
+        cosine = cos_ref[h * RING // 2:(h + 1) * RING // 2].reshape(half_r, HD)
+        sine = sin_ref[h * RING // 2:(h + 1) * RING // 2].reshape(half_r, HD)
+        queries = (q_raw * cosine + pltpu.roll(q_raw, HD // 2, 1) * sine).astype(jnp.bfloat16)
+        keys = kv_all[0].reshape(rows, HD)
+        values = kv_all[1].reshape(rows, HD)
+        scores = lax.dot_general(
+            queries, keys, (((1,), (1,)), ((), ())), preferred_element_type=jnp.float32
+        ) * (HD ** -0.5)
+        allowed = pos_row[lines] <= pos_col[lines]
+        scores = jnp.where(allowed, scores, -1e30)
+        peak = jnp.max(scores, axis=-1, keepdims=True)
+        expo = jnp.where(allowed, jnp.exp(scores - peak), 0.0)
+        weights = (expo / jnp.sum(expo, axis=-1, keepdims=True)).astype(jnp.bfloat16)
+        ctx[h, 0] = jnp.dot(
+            weights, values, preferred_element_type=jnp.float32
+        ).astype(jnp.bfloat16)
+        copy = push(ctx.at[h, 0], ctx.at[h, 1], cp_out.at[h], cp_in.at[h], sibling)
+        sent.append(copy)
+        return copy
+
+    tile = 2 * HD
+
+    def project(h, slot):
+        context = jnp.concatenate([ctx[h, 0], ctx[h, 1]], axis=1)
+        for n in range(width // tile):
+            b, start = divmod(n * tile, half_w)
+            part[h, slot, b, :, start:start + tile] = jnp.dot(
+                context, ow[slot, :, n * tile:(n + 1) * tile], preferred_element_type=jnp.float32
+            )
+
+    def rs_wait(h, i, way):
+        arrived(rs_recv.at[h, way, i], rs_out.at[h, way, i], rs_in.at[h, way, i], way)
+
+    def rs_go(h, i):
+        hop = (i + 1) // 2
+        if i == 0:
+            project(h, RING // 2)
+        elif i % 2:
+            project(h, RING // 2 + hop)
+            project(h, RING // 2 - hop)
+        for way in range(2):
+            slot = RING // 2 + hop if way == 0 else RING // 2 - hop
+            b = (i + way) % 2
+            value = part[h, slot, b]
+            if i >= 2:
+                rs_wait(h, i - 2, way)
+                value += rs_recv[h, way, i - 2].astype(jnp.float32)
+            rs_send[h, way, i] = value.astype(jnp.bfloat16)
+            sent.append(push(
+                rs_send.at[h, way, i], rs_recv.at[h, way, i],
+                rs_out.at[h, way, i], rs_in.at[h, way, i], ways[way],
+            ))
+
+    def rs_end(h):
+        for i in (last - 1, last):
+            for way in range(2):
+                b = (i + way) % 2
+                rs_wait(h, i, way)
+                part[h, 0, b] += rs_recv[h, way, i].astype(jnp.float32)
+        for b in range(2):
+            out_ref[h * half_r:(h + 1) * half_r, b * half_w:(b + 1) * half_w] = (
+                part[h, 0, b].astype(out_ref.dtype)
+            )
+
+    q_pass = q_exchange(0)
+    ag_step(1, 0)
+    q_add(1, 0)
+    kv_pass_in = kv_all.at[1 - core]
+    pltpu.make_async_remote_copy(
+        src_ref=kv_pass_in, dst_ref=kv_pass_in, send_sem=pair_out.at[1], recv_sem=pair_in.at[1],
+        device_id={"head": sibling}, device_id_type=pl.DeviceIdType.MESH,
+    ).wait_recv()
+    ctx_pass = attend(0, q_pass)
+    ag_step(1, 1)
+    q_add(1, 1)
+    for r in range(RING):
+        o_local[r].wait()
+        o_pair[r].wait_recv()
+    ctx_pass.wait_recv()
+    rs_go(0, 0)
+    ag_step(1, 2)
+    rs_go(0, 1)
+    q_add(1, 2)
+    ag_step(1, 3)
+    q_add(1, 3)
+    ag_step(1, 4)
+    rs_go(0, 2)
+    q_add(1, 4)
+    ag_step(1, 5)
+    q_add(1, 5)
+    rs_go(0, 3)
+    ag_step(1, 6)
+    q_add(1, 6)
+    q_pass = q_exchange(1)
+    rs_go(0, 4)
+    ctx_pass = attend(1, q_pass)
+    rs_go(0, 5)
+    ctx_pass.wait_recv()
+    rs_go(1, 0)
+    rs_go(0, 6)
+    rs_go(1, 1)
+    project(0, 0)
+    rs_go(1, 2)
+    rs_go(1, 3)
+    rs_end(0)
+    rs_go(1, 4)
+    rs_go(1, 5)
+    project(1, 0)
+    rs_go(1, 6)
+    rs_end(1)
+    for copy in sent:
+        copy.wait_send()
+
+
+def on_ring(tokens, positions, q_weight, kv_weight, o_weight):
+    rows, width = tokens.shape
+    piece = rows // RING
+    hops = RING - 1
+    any_space = pl.BlockSpec(memory_space=pltpu.HBM)
+    vmem = pl.BlockSpec(memory_space=pltpu.VMEM)
+    bf16, f32 = jnp.bfloat16, jnp.float32
+    dma = pltpu.SemaphoreType.DMA
+    return pl.pallas_call(
+        fused,
+        out_shape=jax.ShapeDtypeStruct((rows, width), bf16),
+        in_specs=[any_space] * 5,
+        out_specs=vmem,
+        scratch_shapes=[
+            pltpu.VMEM((1, rows), jnp.int32),
+            pltpu.VMEM((RING, piece, HD), f32),
+            pltpu.VMEM((RING, piece, HD), f32),
+            pltpu.VMEM((2, RING, 2, rows // 2, width // 2), bf16),
+            pltpu.VMEM((rows, width), bf16),
+            pltpu.VMEM((RING, width, 2 * HD), bf16),
+            pltpu.VMEM((width, 2 * HD), bf16),
+            pltpu.VMEM((RING, 2 * HD, width), bf16),
+            pltpu.VMEM((2, rows // 2, 2 * HD), f32),
+            pltpu.VMEM((2, rows // 2, HD), f32),
+            pltpu.VMEM((2, rows // 2, HD), f32),
+            pltpu.VMEM((2, rows, HD), f32),
+            pltpu.VMEM((rows, HD), f32),
+            pltpu.VMEM((RING, piece, HD), f32),
+            pltpu.VMEM((RING, piece, HD), f32),
+            pltpu.VMEM((2, RING, piece, HD), bf16),
+            pltpu.VMEM((2, 2, rows // 2, HD), bf16),
+            pltpu.VMEM((2, RING, 2, rows // 2, width // 2), f32),
+            pltpu.VMEM((2, 2, hops, rows // 2, width // 2), bf16),
+            pltpu.VMEM((2, 2, hops, rows // 2, width // 2), bf16),
+            dma, dma, dma, dma((RING,)), dma((RING,)), dma((RING,)),
+            dma((RING,)), dma((RING,)), dma((RING,)),
+            dma((2, 2, hops)), dma((2, 2, hops)), dma((2,)), dma((2,)),
+            dma((2,)), dma((2,)), dma((2,)), dma((2,)),
+            dma((RING,)), dma((RING,)), dma((RING,)), dma((RING,)),
+            dma((2, 2, hops)), dma((2, 2, hops)),
+        ],
+        compiler_params=pltpu.CompilerParams(
+            collective_id=0, has_side_effects=True, vmem_limit_bytes=40 * 2**20
+        ),
+        name="prefill_ring",
+    )(
+        positions[None, :], tokens, q_weight.reshape(RING, CORES, width, HD), kv_weight, o_weight,
+    )
+
+
 def solution(mesh):
+    ring = mesh.shape["head"] == RING * CORES
     return jax.shard_map(
-        on_device,
+        on_ring if ring else on_device,
         mesh=mesh,
         in_specs=(P("grp", "head"), P("grp"), P(None, "head"), P("head", None), P("head", None)),
         out_specs=P("grp", "head"),

time: 280 us -> 65 us (0.23)
  waiting for transfers between devices: 247 us -> 0 us
  Pallas kernels: 0 us -> 57 us
  matrix products: 14.2 us -> 0 us
  between operations: 13.2 us -> 0.01 us
  local copies, waits for them, and re-layouts: 2.13 us -> 7.73 us
    reduce_scatter x1 -> x0, waiting for transfers between devices: 103 us -> none  [on_device(): lax.psum_scatter(lax.dot_general(o_weight, context, (((0,), (1,)), ((), (...]
    psum x1 -> x0, waiting for transfers between devices: 89.5 us -> none  [on_device(): kv_raw = lax.psum(partial_value, 'head')]
    pallas_call x0 -> x1, Pallas kernels: none -> 57 us  [on_ring(): pl.pallas_call(fused, out_shape=jax.ShapeDtypeStruct((rows, width), bf16)...]
    all_gather x1 -> x0, waiting for transfers between devices: 53.3 us -> none  [on_device(): lax.all_gather(tokens, 'head', axis=1, tiled=True)]
    dot_general x4 -> x0, matrix products: 14.2 us -> none  [the longest x1 6.95 us: on_device(): lax.dot_general(o_weight, context, (((0,), (1,)), ((), ())), preferred_el...]
    unnamed x6 -> x11, local copies, waits for them, and re-layouts: 1.21 us -> 7.73 us
  transfers between devices with their start and end apart: 3 -> 0, of which waited for: 3 -> 0; matrix products, arithmetic and copies ran while one was open for 1% -> 0% of each run, Pallas kernels for 0% -> 0%
where the time goes in v3:
time: 65 us; the launch traced here: 64.7 us
  Pallas kernels  57 us (88%)
  local copies, waits for them, and re-layouts  7.73 us (12%)
    pallas_call x1, Pallas kernels, on_ring(): pl.pallas_call(fused, out_shape=jax.ShapeDtypeStruct((rows, width), bf16)...  57 us
    unnamed x11, local copies, waits for them, and re-layouts  7.73 us

profile of v3, /device:TPU:0, one launch (start us, length us, event | category | flops | bytes accessed | tf_op | source)
XLA Modules:
  0.0 64.7 jit_solution(2819120549505286190)
XLA Ops:
  0.0 0.0 copy-start
  0.0 2.2 %copy-done = bf16[16384,128]{1,0:T(8,128)(2,1)S(1)} copy-done((bf16[16384,128]{1,0:T(8,128)(2,1)S(1)}, bf16[16384,128]{1,0:T(8,128)(2,1)}, u32[]{:S(2)}) %copy-start) | copy-done | bytes 4194328
  2.2 0.0 copy-start.1
  2.2 2.2 %copy-done.1 = bf16[128,16384]{1,0:T(8,128)(2,1)S(1)} copy-done((bf16[128,16384]{1,0:T(8,128)(2,1)S(1)}, bf16[128,16384]{1,0:T(8,128)(2,1)}, u32[]{:S(2)}) %copy-start.1) | copy-done | bytes 4194328
  4.4 0.0 copy-start.2
  4.4 1.0 %copy-done.2 = bf16[1024,256]{1,0:T(8,128)(2,1)S(1)} copy-done((bf16[1024,256]{1,0:T(8,128)(2,1)S(1)}, bf16[1024,256]{1,0:T(8,128)(2,1)}, u32[]{:S(2)}) %copy-start.2) | copy-done | bytes 524312
  5.4 0.0 copy-start.3
  5.4 0.9 %copy-done.3 = bf16[128,1024]{1,0:T(8,128)(2,1)S(1)} copy-done((bf16[128,1024]{1,0:T(8,128)(2,1)S(1)}, bf16[128,1024]{1,0:T(8,128)(2,1)}, u32[]{:S(2)}) %copy-start.3) | copy-done | bytes 262168
  6.4 0.0 copy-start.4
  6.4 0.7 %copy-done.4 = s32[128]{0:T(128)S(1)} copy-done((s32[128]{0:T(128)S(1)}, s32[128]{0:T(128)}, u32[]{:S(2)}) %copy-start.4) | copy-done | bytes 536
  7.0 57.0 %prefill_ring.1 = bf16[128,1024]{1,0:T(8,128)(2,1)S(1)} custom-call(s32[1,128]{1,0:T(1,128)S(1)} %bitcast.3, bf16[128,1024]{1,0:T(8,128)(2,1)S(1)} %copy-done.3, bf16[8,2,1024,128]{3,2,1,0:T(8,128)(2,1)S(1)} %bitcast.2, bf16[1024,256]{1,0:T(8,128)(2,1)S(1)} %copy-done.2, bf16[128,16384]{1,0:T(8,128)(2,1)S(1)} %copy-done.1), custom_call_target="tpu_custom_call" | custom-call | tf_op jit(solution)/shard_map/prefill_ring/pallas_call | solution.py:397
  64.0 0.7 %copy.7 = bf16[128,1024]{1,0:T(8,128)(2,1)} copy(bf16[128,1024]{1,0:T(8,128)(2,1)S(1)} %prefill_ring.1) | data formatting | bytes 524288
Async XLA Ops:
  0.0 2.2 %copy-start = (bf16[16384,128]{1,0:T(8,128)(2,1)S(1)}, bf16[16384,128]{1,0:T(8,128)(2,1)}, u32[]{:S(2)}) copy-start(bf16[16384,128]{1,0:T(8,128)(2,1)} %param.7) | copy-start | bytes 12582916
  2.2 2.2 %copy-start.1 = (bf16[128,16384]{1,0:T(8,128)(2,1)S(1)}, bf16[128,16384]{1,0:T(8,128)(2,1)}, u32[]{:S(2)}) copy-start(bf16[128,16384]{1,0:T(8,128)(2,1)} %o_hbm.1) | copy-start | bytes 12582916
  4.4 1.0 %copy-start.2 = (bf16[1024,256]{1,0:T(8,128)(2,1)S(1)}, bf16[1024,256]{1,0:T(8,128)(2,1)}, u32[]{:S(2)}) copy-start(bf16[1024,256]{1,0:T(8,128)(2,1)} %kv_hbm.1) | copy-start | bytes 1572868
  5.4 0.9 %copy-start.3 = (bf16[128,1024]{1,0:T(8,128)(2,1)S(1)}, bf16[128,1024]{1,0:T(8,128)(2,1)}, u32[]{:S(2)}) copy-start(bf16[128,1024]{1,0:T(8,128)(2,1)} %tok_hbm.1) | copy-start | bytes 786436
  6.4 0.7 %copy-start.4 = (s32[128]{0:T(128)S(1)}, s32[128]{0:T(128)}, u32[]{:S(2)}) copy-start(s32[128]{0:T(128)} %param.6) | copy-start | bytes 1540

commit v4 on v3

--- a/solution.py
+++ b/solution.py
@@ -428,7 +428,7 @@
             dma((2, 2, hops)), dma((2, 2, hops)),
         ],
         compiler_params=pltpu.CompilerParams(
-            collective_id=0, has_side_effects=True, vmem_limit_bytes=40 * 2**20
+            collective_id=0, has_side_effects=True, vmem_limit_bytes=60 * 2**20
         ),
         name="prefill_ring",
     )(

time: 65 us -> 59.8 us (0.920)
  local copies, waits for them, and re-layouts: 7.73 us -> 1.67 us
  Pallas kernels: 57 us -> 58 us
    unnamed x11 -> x1, local copies, waits for them, and re-layouts: 7.73 us -> 1.67 us
    pallas_call x1, Pallas kernels: 57 us -> 58 us  [on_ring(): pl.pallas_call(fused, out_shape=jax.ShapeDtypeStruct((rows, width), bf16)...]
where the time goes in v4:
time: 59.8 us; the launch traced here: 59.6 us
  Pallas kernels  58 us (97%)
  local copies, waits for them, and re-layouts  1.67 us (3%)
    pallas_call x1, Pallas kernels, on_ring(): pl.pallas_call(fused, out_shape=jax.ShapeDtypeStruct((rows, width), bf16)...  58 us
    unnamed x1, local copies, waits for them, and re-layouts  1.67 us

profile of v4, /device:TPU:0, one launch (start us, length us, event | category | flops | bytes accessed | tf_op | source)
XLA Modules:
  0.0 59.6 jit_solution(6501925526277997263)
XLA Ops:
  0.0 58.0 %prefill_ring.1 = bf16[128,1024]{1,0:T(8,128)(2,1)} custom-call(s32[1,128]{1,0:T(1,128)} %bitcast.3, bf16[128,1024]{1,0:T(8,128)(2,1)} %tok_hbm.1, bf16[8,2,1024,128]{3,2,1,0:T(8,128)(2,1)} %bitcast.2, bf16[1024,256]{1,0:T(8,128)(2,1)} %kv_hbm.1, bf16[128,16384]{1,0:T(8,128)(2,1)} %o_hbm.1), custom_call_target="tpu_custom_call" | custom-call | tf_op jit(solution)/shard_map/prefill_ring/pallas_call | solution.py:397
  58.0 1.7 %copy.7 = bf16[128,1024]{1,0:T(8,128)(2,1)} copy(bf16[128,1024]{1,0:T(8,128)(2,1)} %prefill_ring.1) | data formatting | bytes 524288

commit v5 on v2

--- a/solution.py
+++ b/solution.py
@@ -125,15 +125,11 @@
     kvw_local = pull(kv_hbm, kvw, kvw_sem)
 
     barrier = pltpu.get_barrier_semaphore()
-    for offset in range(RING):
-        for other in range(CORES):
-            if offset or other:
-                pl.semaphore_signal(
-                    barrier, inc=1,
-                    device_id={"head": at(offset, lax.rem(core + other, CORES))},
-                    device_id_type=pl.DeviceIdType.MESH,
-                )
-    pl.semaphore_wait(barrier, RING * CORES - 1)
+    for target in [sibling] + [at(offset, core) for offset in range(1, RING)]:
+        pl.semaphore_signal(
+            barrier, inc=1, device_id={"head": target}, device_id_type=pl.DeviceIdType.MESH
+        )
+    pl.semaphore_wait(barrier, RING)
 
     ways = (right, left)
 
@@ -251,23 +247,29 @@
             is_key = (core == 0).astype(jnp.float32)
             kv_all[core, place] = (turned * is_key + total * (1.0 - is_key)).astype(jnp.bfloat16)
             kv_out = []
-            for r in range(RING):
-                for other in range(CORES):
-                    if r or other:
-                        kv_out.append(push(
-                            kv_all.at[core, place], kv_all.at[core, place],
-                            ka_out.at[other, r], ka_in.at[other, r],
-                            at(r, lax.rem(core + other, CORES)),
-                        ))
+            for r in range(1, RING):
+                kv_out.append(push(
+                    kv_all.at[core, place], kv_all.at[core, place],
+                    ka_out.at[r], ka_in.at[r], at(r, core),
+                ))
             sent += kv_out
+        if i == 5:
+            for copy in kv_out:
+                copy.wait_recv()
+            sent.append(push(
+                kv_all.at[core], kv_all.at[core], pair_out.at[3], pair_in.at[3], sibling
+            ))
         for way in range(2):
             q_add(shard(way, i // 2 + 1), (i + way) % 2)
 
     q_send[...] = q_acc[:, HD:2 * HD]
     q_pass = push(q_send, q_recv, pair_out.at[1], pair_in.at[1], sibling)
     sent.append(q_pass)
-    for copy in kv_out:
-        copy.wait_recv()
+    other_half = kv_all.at[1 - core]
+    pltpu.make_async_remote_copy(
+        src_ref=other_half, dst_ref=other_half, send_sem=pair_out.at[3], recv_sem=pair_in.at[3],
+        device_id={"head": sibling}, device_id_type=pl.DeviceIdType.MESH,
+    ).wait_recv()
     q_pass.wait_recv()
     q_raw = q_acc[:, 0:HD] + q_recv[...]
     cosine = cos_ref[...].reshape(rows, HD)
@@ -375,8 +377,8 @@
             pltpu.VMEM((2, hops, rows // 2, width), bf16),
             dma, dma((2,)), dma, dma((RING,)), dma((RING,)), dma((RING,)),
             dma((RING,)), dma((RING,)), dma((RING,)),
-            dma((2, hops)), dma((2, hops)), dma((3,)), dma((3,)),
-            dma((RING,)), dma((RING,)), dma((2, RING)), dma((2, RING)),
+            dma((2, hops)), dma((2, hops)), dma((4,)), dma((4,)),
+            dma((RING,)), dma((RING,)), dma((RING,)), dma((RING,)),
             dma((2, hops)), dma((2, hops)),
         ],
         compiler_params=pltpu.CompilerParams(

time: 58.3 us -> 56.7 us (0.973)
  Pallas kernels: 56.5 us -> 54.9 us
    pallas_call x1, Pallas kernels: 56.5 us -> 54.9 us  [on_ring(): pl.pallas_call(fused, out_shape=jax.ShapeDtypeStruct((rows, width), bf16)...]
where the time goes in v5:
time: 56.7 us; the launch traced here: 56.6 us
  Pallas kernels  54.9 us (97%)
  local copies, waits for them, and re-layouts  1.67 us (3%)
    pallas_call x1, Pallas kernels, on_ring(): pl.pallas_call(fused, out_shape=jax.ShapeDtypeStruct((rows, width), bf16)...  54.9 us
    unnamed x1, local copies, waits for them, and re-layouts  1.67 us

profile of v5, /device:TPU:0, one launch (start us, length us, event | category | flops | bytes accessed | tf_op | source)
XLA Modules:
  0.0 56.6 jit_solution(3827350636587141864)
XLA Ops:
  0.0 54.9 %prefill_ring.1 = bf16[128,1024]{1,0:T(8,128)(2,1)} custom-call(s32[1,128]{1,0:T(1,128)} %bitcast.3, bf16[128,1024]{1,0:T(8,128)(2,1)} %tok_hbm.1, bf16[8,2,1024,128]{3,2,1,0:T(8,128)(2,1)} %bitcast.2, bf16[1024,256]{1,0:T(8,128)(2,1)} %kv_hbm.1, bf16[128,16384]{1,0:T(8,128)(2,1)} %o_hbm.1), custom_call_target="tpu_custom_call" | custom-call | tf_op jit(solution)/shard_map/prefill_ring/pallas_call | solution.py:353
  54.9 1.7 %copy.7 = bf16[128,1024]{1,0:T(8,128)(2,1)} copy(bf16[128,1024]{1,0:T(8,128)(2,1)} %prefill_ring.1) | data formatting | bytes 524288

commit v6 on v5

--- a/solution.py
+++ b/solution.py
@@ -80,7 +80,7 @@
 
 def fused(
     pos_hbm, tok_hbm, q_hbm, kv_hbm, o_hbm, out_ref, pos, cos_ref, sin_ref,
-    tok, qw, kvw, ow, q_acc, q_send, q_recv, kv_part, kv_sib, kv_sum, kv_in, kv_all,
+    tok, qw, kvw, ow, q_acc, q_send, q_recv, kv_part, kv_sib, kv_sum, kv_side, kv_col, kv_in, kv_all,
     ctx, part, rs_send, rs_recv,
     pos_sem, tok_sem, kvw_sem, q_sem, q_out, q_in, o_sem, o_out, o_in,
     ag_out, ag_in, pair_out, pair_in, kr_out, kr_in, ka_out, ka_in, rs_out, rs_in,
@@ -206,15 +206,26 @@
     step(0)
     kv_pair.wait_recv()
     kv_sum[...] = (kv_part[core] + kv_sib[...]).reshape(RING, piece, HD)
+    quad = RING // 2
+    across = push(
+        kv_sum.at[pl.ds((1 - side) * quad, quad)], kv_side, pair_out.at[4], pair_in.at[4],
+        head_at(RING - 1 - place, core),
+    )
+    sent.append(across)
+
+    step(1)
+    across.wait_recv()
+    kv_col[...] = kv_sum[pl.ds(side * quad, quad)] + kv_side[...]
+    spot = place - side * quad
     kv_rows = []
-    for r in range(1, RING):
-        to = lax.rem(place + r, RING)
+    for r in range(1, quad):
+        to = lax.rem(spot + r, quad)
         kv_rows.append(push(
-            kv_sum.at[to], kv_in.at[r], kr_out.at[r], kr_in.at[r], at(r, core)
+            kv_col.at[to], kv_in.at[r], kr_out.at[r], kr_in.at[r],
+            head_at(side * quad + to, core),
         ))
     sent += kv_rows
 
-    step(1)
     o_local, o_pair = [], []
     for r in range(RING):
         mine = pl.multiple_of(at(-r, core) * width, width)
@@ -238,9 +249,9 @@
 
     for i in range(2, last + 1):
         step(i)
-        if i == 2:
-            total = kv_sum[place]
-            for r in range(1, RING):
+        if i == 3:
+            total = kv_col[spot]
+            for r in range(1, quad):
                 kv_rows[r - 1].wait_recv()
                 total += kv_in[r]
             turned = total * cos_ref[place] + pltpu.roll(total, HD // 2, 1) * sin_ref[place]
@@ -369,6 +380,8 @@
             pltpu.VMEM((2, rows, HD), f32),
             pltpu.VMEM((rows, HD), f32),
             pltpu.VMEM((RING, piece, HD), f32),
+            pltpu.VMEM((RING // 2, piece, HD), f32),
+            pltpu.VMEM((RING // 2, piece, HD), f32),
             pltpu.VMEM((RING, piece, HD), f32),
             pltpu.VMEM((2, RING, piece, HD), bf16),
             pltpu.VMEM((2, rows, HD), bf16),
@@ -377,7 +390,7 @@
             pltpu.VMEM((2, hops, rows // 2, width), bf16),
             dma, dma((2,)), dma, dma((RING,)), dma((RING,)), dma((RING,)),
             dma((RING,)), dma((RING,)), dma((RING,)),
-            dma((2, hops)), dma((2, hops)), dma((4,)), dma((4,)),
+            dma((2, hops)), dma((2, hops)), dma((5,)), dma((5,)),
             dma((RING,)), dma((RING,)), dma((RING,)), dma((RING,)),
             dma((2, hops)), dma((2, hops)),
         ],

time: 56.7 us -> 56.2 us (level)
  no operation moved by 1% of the time
where the time goes in v6:
time: 56.2 us; the launch traced here: 56.1 us
  Pallas kernels  54.4 us (97%)
  local copies, waits for them, and re-layouts  1.67 us (3%)
    pallas_call x1, Pallas kernels, on_ring(): pl.pallas_call(fused, out_shape=jax.ShapeDtypeStruct((rows, width), bf16)...  54.4 us
    unnamed x1, local copies, waits for them, and re-layouts  1.67 us

profile of v6, /device:TPU:0, one launch (start us, length us, event | category | flops | bytes accessed | tf_op | source)
XLA Modules:
  0.0 56.1 jit_solution(12971312725496151059)
XLA Ops:
  0.0 54.4 %prefill_ring.1 = bf16[128,1024]{1,0:T(8,128)(2,1)} custom-call(s32[1,128]{1,0:T(1,128)} %bitcast.3, bf16[128,1024]{1,0:T(8,128)(2,1)} %tok_hbm.1, bf16[8,2,1024,128]{3,2,1,0:T(8,128)(2,1)} %bitcast.2, bf16[1024,256]{1,0:T(8,128)(2,1)} %kv_hbm.1, bf16[128,16384]{1,0:T(8,128)(2,1)} %o_hbm.1), custom_call_target="tpu_custom_call" | custom-call | tf_op jit(solution)/shard_map/prefill_ring/pallas_call | solution.py:364
  54.4 1.7 %copy.7 = bf16[128,1024]{1,0:T(8,128)(2,1)} copy(bf16[128,1024]{1,0:T(8,128)(2,1)} %prefill_ring.1) | data formatting | bytes 524288
